TPU v7x, 256 devices: a whole 4x4x8 slice. The times are simulated.
256 devices in a mesh: shape: 4 (over y), space: 64 (over x, z, core).
Axes of the slice: x: 4, y: 4, z: 8, core: 2. Of those that a mesh axis runs over, the one named last changes fastest.
Arguments:
- features: bfloat16 [4, 128, 512, 128], P('shape', 'space'), may hold values from -45 to 45
- gain_one: float32 [128], replicated, may hold values from 0.1 to 1.9
- weight_one: bfloat16 [7, 128, 128], replicated, may hold values from -0.1875 to 0.1875
- gain_two: float32 [128], replicated, may hold values from 0.1 to 1.9
- weight_two: bfloat16 [7, 128, 128], replicated, may hold values from -0.1875 to 0.1875
- live: int32 [4, 128], P('shape', 'space'), may hold values from 0 to 1, as said below
- send_index: int32 [4, 64, 64, 1], P('shape', 'space'), may hold values from -1 to 11, as said below
- recv_index: int32 [4, 128, 6], P('shape', 'space'), may hold values from -1 to 63, as said below
- cotangent: bfloat16 [4, 128, 512, 128], P('shape', 'space'), may hold values from -6 to 6
Outputs:
- output: bfloat16 [4, 128, 512, 128], P('shape', 'space')
- grad_features: bfloat16 [4, 128, 512, 128], P('shape', 'space')
- grad_weight_one: float32 [7, 128, 128], replicated
- grad_weight_two: float32 [7, 128, 128], replicated
- grad_gain_one: float32 [128], replicated
- grad_gain_two: float32 [128], replicated
Inputs may be any that keep to these rules, and one draw needn't show every extreme that they name: The live slots of each device are its first ones, at least 1 of them; in every shape one device has both slots live and another only 1. `recv_index`: -1 where the face has no neighbour slab, always so on slots that are not live; else a position r of the device's receive buffer of 64 slabs, r being the sending device (one slab per sender). No two faces of one device share a position; on every device the slot from some sender is in use; slot 0 of every device has all six faces. send_index[s, d, e, c] is -1 where slot c from device d to device e is unused, else 6 b + f for a live slot b of device d, f being the opposite of the face of the brick of e that reads that slot; it agrees with recv_index.
All inputs are finite; a program needn't handle non-finite values.
Results may differ from a plain program's by a relative error of at most 0.014.
Values may be sent and summed in bfloat16 or wider, within the bound.
A program may use at most 64 MiB of HBM per device.

v0:
```python
import math
import jax
import jax.numpy as jnp
from jax import lax
from jax.sharding import PartitionSpec as P

EDGE = 8
OFFSETS = ((0, 0, 0), (-1, 0, 0), (1, 0, 0), (0, -1, 0), (0, 1, 0), (0, 0, -1), (0, 0, 1))
norm_epsilon = 1e-05


def pre_act(values, gain):
    row_mean = jnp.mean(values, axis=-1, keepdims=True)
    centered = values - row_mean
    variance = jnp.mean(centered * centered, axis=-1, keepdims=True)
    return jax.nn.silu(centered * lax.rsqrt(variance + norm_epsilon) * gain)


def pre_back(brick_cube, gain, upstream):
    outputs, pullback = jax.vjp(pre_act, brick_cube.astype(jnp.float32), gain)
    return pullback(upstream)


def face_slabs(brick_cube):
    brick_count = brick_cube.shape[0]
    edge_len = brick_cube.shape[1]
    last_layer = edge_len - 1
    face_list = [
        brick_cube[:, 0],
        brick_cube[:, last_layer],
        brick_cube[:, :, 0],
        brick_cube[:, :, last_layer],
        brick_cube[:, :, :, 0],
        brick_cube[:, :, :, last_layer],
    ]
    return jnp.stack(
        [
            face_part.reshape(brick_count, edge_len * edge_len, brick_cube.shape[-1])
            for face_part in face_list
        ],
        axis=1,
    )


def pad_cube(brick_cube, halo_slabs):
    brick_count = brick_cube.shape[0]
    edge_len = brick_cube.shape[1]
    channels = brick_cube.shape[-1]
    slab_grid = halo_slabs.reshape(brick_count, 6, edge_len, edge_len, channels)
    far_side = edge_len + 1
    inside = slice(1, far_side)
    padded = jnp.pad(brick_cube, ((0, 0), (1, 1), (1, 1), (1, 1), (0, 0)))
    padded = padded.at[:, 0, inside, inside].set(slab_grid[:, 0])
    padded = padded.at[:, far_side, inside, inside].set(slab_grid[:, 1])
    padded = padded.at[:, inside, 0, inside].set(slab_grid[:, 2])
    padded = padded.at[:, inside, far_side, inside].set(slab_grid[:, 3])
    padded = padded.at[:, inside, inside, 0].set(slab_grid[:, 4])
    padded = padded.at[:, inside, inside, far_side].set(slab_grid[:, 5])
    return padded


def add_faces(volume, face_terms):
    brick_count = volume.shape[0]
    edge_len = volume.shape[1]
    channels = volume.shape[-1]
    term_grid = face_terms.reshape(brick_count, 6, edge_len, edge_len, channels)
    last_layer = edge_len - 1
    volume = volume.at[:, 0].add(term_grid[:, 0])
    volume = volume.at[:, last_layer].add(term_grid[:, 1])
    volume = volume.at[:, :, 0].add(term_grid[:, 2])
    volume = volume.at[:, :, last_layer].add(term_grid[:, 3])
    volume = volume.at[:, :, :, 0].add(term_grid[:, 4])
    volume = volume.at[:, :, :, last_layer].add(term_grid[:, 5])
    return volume


def shifted(padded, tap_index):
    step_i, step_j, step_k = OFFSETS[tap_index]
    edge_len = padded.shape[1] - 2
    window = padded[
        :,
        1 + step_i : 1 + step_i + edge_len,
        1 + step_j : 1 + step_j + edge_len,
        1 + step_k : 1 + step_k + edge_len,
    ]
    return window.reshape(-1, padded.shape[-1])


def convolve(padded, weight):
    running = jnp.dot(shifted(padded, 0), weight[0], preferred_element_type=jnp.float32)
    for tap_index in range(1, len(OFFSETS)):
        running = running + jnp.dot(
            shifted(padded, tap_index), weight[tap_index], preferred_element_type=jnp.float32
        )
    return running


def conv_back(padded, grad_rows, weight):
    brick_count = padded.shape[0]
    edge_len = padded.shape[1] - 2
    channels = padded.shape[-1]
    weight_grad = jnp.stack(
        [
            lax.dot_general(
                shifted(padded, tap_index),
                grad_rows,
                (((0,), (0,)), ((), ())),
                preferred_element_type=jnp.float32,
            )
            for tap_index in range(len(OFFSETS))
        ]
    )
    spread = jnp.zeros(padded.shape, jnp.float32)
    for tap_index in range(len(OFFSETS)):
        step_i, step_j, step_k = OFFSETS[tap_index]
        tap_term = lax.dot_general(
            grad_rows,
            weight[tap_index],
            (((1,), (1,)), ((), ())),
            preferred_element_type=jnp.float32,
        )
        tap_term = tap_term.reshape(brick_count, edge_len, edge_len, edge_len, channels)
        spread = spread.at[
            :,
            1 + step_i : 1 + step_i + edge_len,
            1 + step_j : 1 + step_j + edge_len,
            1 + step_k : 1 + step_k + edge_len,
        ].add(tap_term)
    far_side = edge_len + 1
    inside = slice(1, far_side)
    interior = spread[:, inside, inside, inside]
    face_list = [
        spread[:, 0, inside, inside],
        spread[:, far_side, inside, inside],
        spread[:, inside, 0, inside],
        spread[:, inside, far_side, inside],
        spread[:, inside, inside, 0],
        spread[:, inside, inside, far_side],
    ]
    halo_grad = jnp.stack(
        [face_part.reshape(brick_count, edge_len * edge_len, channels) for face_part in face_list],
        axis=1,
    ).astype(jnp.bfloat16)
    return (weight_grad, interior, halo_grad)


def trade_faces(brick_cube, send_pick, recv_pick, peer_count, slot_count):
    face_rows = face_slabs(brick_cube)
    flat_rows = face_rows.reshape(send_pick.shape[1], -1)
    outgoing = jnp.dot(send_pick, flat_rows, preferred_element_type=jnp.float32).astype(
        jnp.bfloat16
    )
    incoming = lax.all_to_all(
        outgoing.reshape(peer_count, slot_count, -1),
        "space",
        split_axis=0,
        concat_axis=0,
        tiled=True,
    )
    halo_slabs = jnp.dot(
        recv_pick, incoming.reshape(peer_count * slot_count, -1), preferred_element_type=jnp.float32
    ).astype(jnp.bfloat16)
    return halo_slabs.reshape(face_rows.shape)


def return_slabs(halo_grad, send_pick, recv_pick, peer_count, slot_count):
    flat_rows = halo_grad.reshape(recv_pick.shape[0], -1)
    outgoing = lax.dot_general(
        recv_pick, flat_rows, (((0,), (0,)), ((), ())), preferred_element_type=jnp.float32
    ).astype(jnp.bfloat16)
    incoming = lax.all_to_all(
        outgoing.reshape(peer_count, slot_count, -1),
        "space",
        split_axis=0,
        concat_axis=0,
        tiled=True,
    )
    summed = lax.dot_general(
        send_pick,
        incoming.reshape(peer_count * slot_count, -1),
        (((0,), (0,)), ((), ())),
        preferred_element_type=jnp.float32,
    )
    return summed.reshape(halo_grad.shape)


def forward_conv(brick_cube, weight, send_pick, recv_pick, peer_count, slot_count):
    halo_slabs = trade_faces(brick_cube, send_pick, recv_pick, peer_count, slot_count)
    padded = pad_cube(brick_cube, halo_slabs)
    result = convolve(padded, weight).reshape(brick_cube.shape)
    return (result, padded)


def shards(
    features, gain_one, weight_one, gain_two, weight_two, live, send_index, recv_index, cotangent
):
    brick_count = features.shape[1]
    channels = features.shape[3]
    edge_len = EDGE
    peer_count = lax.axis_size("space")
    slot_count = send_index.shape[3]
    cube_shape = (brick_count, edge_len, edge_len, edge_len, channels)
    cubes_in = features.reshape(cube_shape)
    cot_cube = cotangent.reshape(cube_shape)
    alive_rows = (live.reshape(brick_count) > 0)[:, None, None, None, None]
    send_codes = send_index.reshape(peer_count * slot_count)
    places = recv_index.reshape(brick_count * 6)
    send_pick = (
        send_codes[:, None] == jnp.arange(brick_count * 6, dtype=jnp.int32)[None, :]
    ).astype(jnp.bfloat16)
    recv_pick = (
        places[:, None] == jnp.arange(peer_count * slot_count, dtype=jnp.int32)[None, :]
    ).astype(jnp.bfloat16)
    acts_one = pre_act(cubes_in.astype(jnp.float32), gain_one).astype(jnp.bfloat16)
    conv_one, padded_one = forward_conv(
        acts_one, weight_one, send_pick, recv_pick, peer_count, slot_count
    )
    hidden = conv_one.astype(jnp.bfloat16)
    acts_two = pre_act(hidden.astype(jnp.float32), gain_two).astype(jnp.bfloat16)
    conv_two, padded_two = forward_conv(
        acts_two, weight_two, send_pick, recv_pick, peer_count, slot_count
    )
    output = jnp.where(
        alive_rows, cubes_in.astype(jnp.float32) + conv_two, jnp.zeros(conv_two.shape, jnp.float32)
    ).astype(jnp.bfloat16)
    grad_rows = jnp.where(alive_rows, cot_cube, jnp.zeros_like(cot_cube))
    weight_grad_two, interior_two, halo_grad_two = conv_back(
        padded_two, grad_rows.reshape(-1, channels), weight_two
    )
    returned_two = return_slabs(halo_grad_two, send_pick, recv_pick, peer_count, slot_count)
    grad_hidden, gain_grad_two = pre_back(hidden, gain_two, add_faces(interior_two, returned_two))
    grad_hidden = grad_hidden.astype(jnp.bfloat16)
    weight_grad_one, interior_one, halo_grad_one = conv_back(
        padded_one, grad_hidden.reshape(-1, channels), weight_one
    )
    returned_one = return_slabs(halo_grad_one, send_pick, recv_pick, peer_count, slot_count)
    grad_input, gain_grad_one = pre_back(cubes_in, gain_one, add_faces(interior_one, returned_one))
    direct = jnp.where(
        alive_rows, cot_cube.astype(jnp.float32), jnp.zeros(grad_input.shape, jnp.float32)
    )
    grad_features = (direct + grad_input).astype(jnp.bfloat16)
    weight_sum_one, weight_sum_two, gain_sum_one, gain_sum_two = lax.psum(
        (weight_grad_one, weight_grad_two, gain_grad_one, gain_grad_two), ("shape", "space")
    )
    total_rows = (
        features.shape[0] * lax.axis_size("shape") * brick_count * peer_count * features.shape[2]
    )
    grad_scale = 1.0 / math.sqrt(total_rows)
    return (
        output.reshape(features.shape),
        grad_features.reshape(features.shape),
        weight_sum_one * grad_scale,
        weight_sum_two * grad_scale,
        gain_sum_one * grad_scale,
        gain_sum_two * grad_scale,
    )


def solution(mesh):
    in_specs = (
        P("shape", "space", None, None),
        P(),
        P(),
        P(),
        P(),
        P("shape", "space"),
        P("shape", "space", None, None),
        P("shape", "space", None),
        P("shape", "space", None, None),
    )
    out_specs = (
        P("shape", "space", None, None),
        P("shape", "space", None, None),
        P(),
        P(),
        P(),
        P(),
    )
    return jax.shard_map(shards, mesh=mesh, in_specs=in_specs, out_specs=out_specs, check_vma=False)
```

profile of v0, /device:TPU:4, one launch (start us, length us, event | category | flops | bytes accessed | tf_op | source)
XLA Modules:
  0.0 569.2 jit_solution(17979509776324319021)
XLA Ops:
  16.4 12.4 %all-to-all-start = ((bf16[64,2,4096]{2,1,0:T(2,128)(2,1)}), bf16[64,2,4096]{2,1,0:T(2,128)(2,1)}, u32[]{:S(2)}, u32[]{:S(2)}) async-start(bf16[64,2,4096]{2,1,0:T(2,128)(2,1)} %reshape.1985), calls=%async_computation | async-start | bytes 2097152 | tf_op jit(solution)/shard_map/all_to_all | solution.py:153
  31.3 2.7 scatter-add.89
  34.3 2.7 scatter-add.90
  37.2 2.7 scatter-add.91
  40.1 2.7 scatter-add.94
  43.3 2.7 scatter-add.96
  54.3 3.3 reduce.80
  60.2 11.2 %all-to-all-start.2 = ((bf16[64,2,4096]{2,1,0:T(2,128)(2,1)}), bf16[64,2,4096]{2,1,0:T(2,128)(2,1)}, u32[]{:S(2)}, u32[]{:S(2)}) async-start(bf16[64,2,4096]{2,1,0:T(2,128)(2,1)} %reshape.1989), calls=%async_computation.2 | async-start | bytes 2097152 | tf_op jit(solution)/shard_map/all_to_all | solution.py:171
  71.4 7.5 %reshape.1986 = bf16[64,1,8192]{2,1,0:T(2,128)(2,1)} reshape(bf16[64,2,4096]{2,1,0:T(2,128)(2,1)} %all-to-all-done) | data formatting | bytes 2097152
  78.9 2.8 convolution_convert_fusion.5
  88.9 8.9 %all-to-all-done.2 = bf16[64,2,4096]{2,1,0:T(2,128)(2,1)} async-done(((bf16[64,2,4096]{2,1,0:T(2,128)(2,1)}), bf16[64,2,4096]{2,1,0:T(2,128)(2,1)}, u32[]{:S(2)}, u32[]{:S(2)}) %all-to-all-start.2) | async-done | bytes 1048608 | tf_op jit(solution)/shard_map/all_to_all | solution.py:171
  97.8 7.5 %reshape.1990 = bf16[64,1,8192]{2,1,0:T(2,128)(2,1)} reshape(bf16[64,2,4096]{2,1,0:T(2,128)(2,1)} %all-to-all-done.2) | data formatting | bytes 2097152
  105.3 2.7 copy.213
  118.6 2.9 scatter-add.111
  137.7 8.3 %all-to-all-start.3 = ((bf16[64,2,4096]{2,1,0:T(2,128)(2,1)}), bf16[64,2,4096]{2,1,0:T(2,128)(2,1)}, u32[]{:S(2)}, u32[]{:S(2)}) async-start(bf16[64,2,4096]{2,1,0:T(2,128)(2,1)} %reshape.1991), calls=%async_computation.3 | async-start | bytes 2097152 | tf_op jit(solution)/shard_map/all_to_all | solution.py:171
  152.0 3.3 reduce.82
  164.6 7.9 %all-to-all-done.3 = bf16[64,2,4096]{2,1,0:T(2,128)(2,1)} async-done(((bf16[64,2,4096]{2,1,0:T(2,128)(2,1)}), bf16[64,2,4096]{2,1,0:T(2,128)(2,1)}, u32[]{:S(2)}, u32[]{:S(2)}) %all-to-all-start.3) | async-done | bytes 1048608 | tf_op jit(solution)/shard_map/all_to_all | solution.py:171
  172.6 8.3 %all-to-all-start.1 = ((bf16[64,2,4096]{2,1,0:T(2,128)(2,1)}), bf16[64,2,4096]{2,1,0:T(2,128)(2,1)}, u32[]{:S(2)}, u32[]{:S(2)}) async-start(bf16[64,2,4096]{2,1,0:T(2,128)(2,1)} %reshape.1987), calls=%async_computation.1 | async-start | bytes 2097152 | tf_op jit(solution)/shard_map/all_to_all | solution.py:153
  183.1 7.5 %reshape.1992 = bf16[64,1,8192]{2,1,0:T(2,128)(2,1)} reshape(bf16[64,2,4096]{2,1,0:T(2,128)(2,1)} %all-to-all-done.3) | data formatting | bytes 2097152
  190.6 2.7 copy.212
  197.5 10.0 %all-to-all-done.1 = bf16[64,2,4096]{2,1,0:T(2,128)(2,1)} async-done(((bf16[64,2,4096]{2,1,0:T(2,128)(2,1)}), bf16[64,2,4096]{2,1,0:T(2,128)(2,1)}, u32[]{:S(2)}, u32[]{:S(2)}) %all-to-all-start.1) | async-done | bytes 1048608 | tf_op jit(solution)/shard_map/all_to_all | solution.py:153
  207.5 6.5 %reshape.1988 = bf16[64,1,8192]{2,1,0:T(2,128)(2,1)S(1)} reshape(bf16[64,2,4096]{2,1,0:T(2,128)(2,1)} %all-to-all-done.1) | data formatting | bytes 2097152
  232.3 76.4 %all-reduce.4 = (f32[128]{0:T(128)S(1)}, f32[128]{0:T(128)S(1)}) all-reduce(f32[128]{0:T(128)S(1)} %get-tuple-element.462, f32[128]{0:T(128)S(1)} %get-tuple-element.464), channel_id=1, replica_groups=mesh['shape'=4,'space'=64] {'shape','space'}, use_global_device_ids=true, to_apply=%region_11.12 | all-reduce | flops 256 | bytes 2048 | tf_op jit(solution)/shard_map/psum | solution.py:242
  310.6 249.3 %all-reduce.8.cloned.1.call-done = (f32[7,128,128]{2,1,0:T(8,128)}, f32[7,128,128]{2,1,0:T(8,128)}) async-done(((f32[7,128,128]{2,1,0:T(8,128)}, f32[7,128,128]{2,1,0:T(8,128)}), (f32[7,128,128]{2,1,0:T(8,128)}, f32[7,128,128]{2,1,0:T(8,128)})) %all-reduce.8.cloned.1.call-update) | async-done | bytes 917520 | tf_op jit(solution)/shard_map/psum | solution.py:242
  (252 shorter events, 100.7 us)
Async XLA Ops:
  9.7 2.7 copy-start.4
  9.8 2.3 copy-start.21
  9.8 2.5 copy-start.6
  9.9 2.5 copy-start.26
  16.4 12.6 %copy-start.30 = (s32[1,2]{1,0:T(1,128)S(1)}, s32[1,2]{1,0:T(1,128)}, u32[]{:S(2)}) copy-start(s32[1,2]{1,0:T(1,128)} %param.90) | copy-start | bytes 28
  16.4 12.6 %copy-start.10 = (bf16[1,2,512,128]{3,2,1,0:T(8,128)(2,1)S(1)}, bf16[1,2,512,128]{3,2,1,0:T(8,128)(2,1)}, u32[]{:S(2)}) copy-start(bf16[1,2,512,128]{3,2,1,0:T(8,128)(2,1)} %param.93) | copy-start | bytes 786436
  16.4 43.8 %all-to-all-start = ((bf16[64,2,4096]{2,1,0:T(2,128)(2,1)}), bf16[64,2,4096]{2,1,0:T(2,128)(2,1)}, u32[]{:S(2)}, u32[]{:S(2)}) async-start(bf16[64,2,4096]{2,1,0:T(2,128)(2,1)} %reshape.1985), calls=%async_computation | async-start | bytes 2097152 | tf_op jit(solution)/shard_map/all_to_all | solution.py:153
  31.1 2.9 copy-start.17
  46.7 5.7 %copy-start.23 = (bf16[2,8,8,1,128]{4,3,2,1,0:T(2,128)(2,1)S(1)}, bf16[2,8,8,1,128]{4,3,2,1,0:T(2,128)(2,1)}, u32[]{:S(2)}) copy-start(bf16[2,8,8,1,128]{4,3,2,1,0:T(2,128)(2,1)} %slice.2143) | copy-start | bytes 98308
  60.2 37.6 %all-to-all-start.2 = ((bf16[64,2,4096]{2,1,0:T(2,128)(2,1)}), bf16[64,2,4096]{2,1,0:T(2,128)(2,1)}, u32[]{:S(2)}, u32[]{:S(2)}) async-start(bf16[64,2,4096]{2,1,0:T(2,128)(2,1)} %reshape.1989), calls=%async_computation.2 | async-start | bytes 2097152 | tf_op jit(solution)/shard_map/all_to_all | solution.py:171
  88.4 24.1 %copy-start.13 = (f32[2,8,8,8]{3,2,1,0:T(8,128)}, f32[2,8,8,8]{3,2,1,0:T(8,128)S(1)}, u32[]{:S(2)}) copy-start(f32[2,8,8,8]{3,2,1,0:T(8,128)S(1)} %div.59) | copy-start | bytes 12292
  88.9 23.7 %copy-start.14 = (f32[2,8,8,8]{3,2,1,0:T(8,128)}, f32[2,8,8,8]{3,2,1,0:T(8,128)S(1)}, u32[]{:S(2)}) copy-start(f32[2,8,8,8]{3,2,1,0:T(8,128)S(1)} %rsqrt.23) | copy-start | bytes 12292
  108.3 3.8 copy-start.28
  137.7 34.8 %all-to-all-start.3 = ((bf16[64,2,4096]{2,1,0:T(2,128)(2,1)}), bf16[64,2,4096]{2,1,0:T(2,128)(2,1)}, u32[]{:S(2)}, u32[]{:S(2)}) async-start(bf16[64,2,4096]{2,1,0:T(2,128)(2,1)} %reshape.1991), calls=%async_computation.3 | async-start | bytes 2097152 | tf_op jit(solution)/shard_map/all_to_all | solution.py:171
  146.0 2.1 copy-start.25
  146.0 2.8 copy-start.24
  158.0 2.0 copy-start.1
  172.6 34.9 %all-to-all-start.1 = ((bf16[64,2,4096]{2,1,0:T(2,128)(2,1)}), bf16[64,2,4096]{2,1,0:T(2,128)(2,1)}, u32[]{:S(2)}, u32[]{:S(2)}) async-start(bf16[64,2,4096]{2,1,0:T(2,128)(2,1)} %reshape.1987), calls=%async_computation.1 | async-start | bytes 2097152 | tf_op jit(solution)/shard_map/all_to_all | solution.py:153
  180.9 379.1 %all-reduce.8.cloned.1.call-start = ((), (), s32[]{:S(2)}) async-start(), calls=%async_computation.4 | async-start | bytes 1835008 | tf_op jit(solution)/shard_map/psum | solution.py:242
  226.6 2.9 copy-start.18
  226.7 3.0 copy-start.9
  230.8 78.5 %copy-start.12 = (bf16[1,2,512,128]{3,2,1,0:T(8,128)(2,1)S(1)}, bf16[1,2,512,128]{3,2,1,0:T(8,128)(2,1)}, u32[]{:S(2)}) copy-start(bf16[1,2,512,128]{3,2,1,0:T(8,128)(2,1)} %param.93) | copy-start | bytes 786436
  230.8 78.5 %copy-start.20 = (f32[2,8,8,8]{3,2,1,0:T(8,128)S(1)}, f32[2,8,8,8]{3,2,1,0:T(8,128)}, u32[]{:S(2)}) copy-start(f32[2,8,8,8]{3,2,1,0:T(8,128)} %copy-done.19) | copy-start | bytes 12292
  230.8 78.5 %copy-start.22 = (f32[2,8,8,8]{3,2,1,0:T(8,128)S(1)}, f32[2,8,8,8]{3,2,1,0:T(8,128)}, u32[]{:S(2)}) copy-start(f32[2,8,8,8]{3,2,1,0:T(8,128)} %negate_multiply_fusion) | copy-start | bytes 12292
  (12 other events, 14.6 us)
Sparse Core Ops, SparseCore 0:
  308.8 251.0 all-reduce.7
where the time goes:
time: 579 us; the launch traced here: 569 us
  waiting for transfers between devices  276 us (48%)
  local copies, waits for them, and re-layouts  101 us (17%)
  blocking collectives  76.4 us (13%)
  starting transfers between devices  40.2 us (7%)
  matrix products  32.7 us (6%)
  other arithmetic  27.2 us (5%)
  between operations  15.6 us (3%)
    psum x1, waiting for transfers between devices, shards(): lax.psum((weight_grad_one, weight_grad_two, gain_grad_one, gain_grad_two)...  249 us
    psum x1, blocking collectives, shards(): lax.psum((weight_grad_one, weight_grad_two, gain_grad_one, gain_grad_two)...  76.4 us
    unnamed x106, local copies, waits for them, and re-layouts  53.6 us
    scatter-add x12, local copies, waits for them, and re-layouts, conv_back(): spread = spread.at[:, 1 + step_i:1 + step_i + edge_len, 1 + step_j:1 + st...  27.4 us
    all_to_all x2, starting transfers between devices, trade_faces(): lax.all_to_all(outgoing.reshape(peer_count, slot_count, -1), 'space', spl...  20.7 us
    all_to_all x2, starting transfers between devices, return_slabs(): lax.all_to_all(outgoing.reshape(peer_count, slot_count, -1), 'space', spl...  19.4 us
    all_to_all x2, waiting for transfers between devices, return_slabs(): lax.all_to_all(outgoing.reshape(peer_count, slot_count, -1), 'space', spl...  16.8 us
    dot_general x14, matrix products, conv_back(): lax.dot_general(shifted(padded, tap_index), grad_rows, (((0,), (0,)), (()...  15.3 us
  transfers between devices with their start and end apart: 5, of which 4 were waited for; matrix products, arithmetic and copies ran while one was open for 15% of the time, Pallas kernels for 0%

commit v1 on v0

--- a/solution.py
+++ b/solution.py
@@ -240,7 +240,7 @@
     )
     grad_features = (direct + grad_input).astype(jnp.bfloat16)
     weight_sum_one, weight_sum_two, gain_sum_one, gain_sum_two = lax.psum(
-        (weight_grad_one, weight_grad_two, gain_grad_one, gain_grad_two), ("shape", "space")
+        lax.psum((weight_grad_one, weight_grad_two, gain_grad_one, gain_grad_two), "space"), "shape"
     )
     total_rows = (
         features.shape[0] * lax.axis_size("shape") * brick_count * peer_count * features.shape[2]

time: 579 us -> 615 us (1.062)
  blocking collectives: 76.4 us -> 117 us
    psum x1, waiting for transfers between devices: 249 us -> 195 us  [shards(): lax.psum((weight_grad_one, weight_grad_two, gain_grad_one, gain_grad_two)...]
    psum x0 -> x1, waiting for transfers between devices: none -> 47.8 us  [shards(): lax.psum(lax.psum((weight_grad_one, weight_grad_two, gain_grad_one, gain_...]
    psum x1, blocking collectives: 76.4 us -> 107 us  [shards(): lax.psum((weight_grad_one, weight_grad_two, gain_grad_one, gain_grad_two)...]
    psum x0 -> x1, blocking collectives: none -> 10.7 us  [shards(): lax.psum(lax.psum((weight_grad_one, weight_grad_two, gain_grad_one, gain_...]
    unnamed x106 -> x104, local copies, waits for them, and re-layouts: 53.6 us -> 53.4 us
  transfers between devices with their start and end apart: 5 -> 6, of which waited for: 4 -> 5; matrix products, arithmetic and copies ran while one was open for 15% -> 14% of each run, Pallas kernels for 0% -> 0%
where the time goes in v1:
time: 615 us; the launch traced here: 605 us
  waiting for transfers between devices  270 us (44%)
  blocking collectives  117 us (19%)
  local copies, waits for them, and re-layouts  101 us (16%)
  starting transfers between devices  40.2 us (7%)
  matrix products  33.7 us (5%)
  other arithmetic  27.1 us (4%)
  between operations  15.5 us (3%)
    psum x1, waiting for transfers between devices, shards(): lax.psum((weight_grad_one, weight_grad_two, gain_grad_one, gain_grad_two)...  195 us
    psum x1, blocking collectives, shards(): lax.psum((weight_grad_one, weight_grad_two, gain_grad_one, gain_grad_two)...  107 us
    unnamed x104, local copies, waits for them, and re-layouts  53.4 us
    psum x1, waiting for transfers between devices, shards(): lax.psum(lax.psum((weight_grad_one, weight_grad_two, gain_grad_one, gain_...  47.8 us
    scatter-add x12, local copies, waits for them, and re-layouts, conv_back(): spread = spread.at[:, 1 + step_i:1 + step_i + edge_len, 1 + step_j:1 + st...  27.4 us
    all_to_all x2, starting transfers between devices, trade_faces(): lax.all_to_all(outgoing.reshape(peer_count, slot_count, -1), 'space', spl...  20.7 us
    all_to_all x2, starting transfers between devices, return_slabs(): lax.all_to_all(outgoing.reshape(peer_count, slot_count, -1), 'space', spl...  19.5 us
    all_to_all x2, waiting for transfers between devices, return_slabs(): lax.all_to_all(outgoing.reshape(peer_count, slot_count, -1), 'space', spl...  16.9 us
  transfers between devices with their start and end apart: 6, of which 5 were waited for; matrix products, arithmetic and copies ran while one was open for 14% of the time, Pallas kernels for 0%

profile of v1, /device:TPU:4, one launch (start us, length us, event | category | flops | bytes accessed | tf_op | source)
XLA Modules:
  0.0 604.6 jit_solution(5704650487026730836)
XLA Ops:
  16.4 12.4 %all-to-all-start = ((bf16[64,2,4096]{2,1,0:T(2,128)(2,1)}), bf16[64,2,4096]{2,1,0:T(2,128)(2,1)}, u32[]{:S(2)}, u32[]{:S(2)}) async-start(bf16[64,2,4096]{2,1,0:T(2,128)(2,1)} %reshape.1985), calls=%async_computation | async-start | bytes 2097152 | tf_op jit(solution)/shard_map/all_to_all | solution.py:153
  31.3 2.7 scatter-add.89
  37.2 2.7 scatter-add.91
  40.1 2.7 scatter-add.94
  54.2 3.3 reduce.80
  60.2 11.2 %all-to-all-start.2 = ((bf16[64,2,4096]{2,1,0:T(2,128)(2,1)}), bf16[64,2,4096]{2,1,0:T(2,128)(2,1)}, u32[]{:S(2)}, u32[]{:S(2)}) async-start(bf16[64,2,4096]{2,1,0:T(2,128)(2,1)} %reshape.1989), calls=%async_computation.2 | async-start | bytes 2097152 | tf_op jit(solution)/shard_map/all_to_all | solution.py:171
  71.4 7.5 %reshape.1986 = bf16[64,1,8192]{2,1,0:T(2,128)(2,1)} reshape(bf16[64,2,4096]{2,1,0:T(2,128)(2,1)} %all-to-all-done) | data formatting | bytes 2097152
  78.9 2.8 convolution_convert_fusion.5
  88.8 8.9 %all-to-all-done.2 = bf16[64,2,4096]{2,1,0:T(2,128)(2,1)} async-done(((bf16[64,2,4096]{2,1,0:T(2,128)(2,1)}), bf16[64,2,4096]{2,1,0:T(2,128)(2,1)}, u32[]{:S(2)}, u32[]{:S(2)}) %all-to-all-start.2) | async-done | bytes 1048608 | tf_op jit(solution)/shard_map/all_to_all | solution.py:171
  97.7 7.5 %reshape.1990 = bf16[64,1,8192]{2,1,0:T(2,128)(2,1)} reshape(bf16[64,2,4096]{2,1,0:T(2,128)(2,1)} %all-to-all-done.2) | data formatting | bytes 2097152
  105.2 2.7 copy.213
  118.5 2.9 scatter-add.111
  137.7 8.3 %all-to-all-start.3 = ((bf16[64,2,4096]{2,1,0:T(2,128)(2,1)}), bf16[64,2,4096]{2,1,0:T(2,128)(2,1)}, u32[]{:S(2)}, u32[]{:S(2)}) async-start(bf16[64,2,4096]{2,1,0:T(2,128)(2,1)} %reshape.1991), calls=%async_computation.3 | async-start | bytes 2097152 | tf_op jit(solution)/shard_map/all_to_all | solution.py:171
  152.0 3.3 reduce.82
  164.6 7.9 %all-to-all-done.3 = bf16[64,2,4096]{2,1,0:T(2,128)(2,1)} async-done(((bf16[64,2,4096]{2,1,0:T(2,128)(2,1)}), bf16[64,2,4096]{2,1,0:T(2,128)(2,1)}, u32[]{:S(2)}, u32[]{:S(2)}) %all-to-all-start.3) | async-done | bytes 1048608 | tf_op jit(solution)/shard_map/all_to_all | solution.py:171
  172.5 8.3 %all-to-all-start.1 = ((bf16[64,2,4096]{2,1,0:T(2,128)(2,1)}), bf16[64,2,4096]{2,1,0:T(2,128)(2,1)}, u32[]{:S(2)}, u32[]{:S(2)}) async-start(bf16[64,2,4096]{2,1,0:T(2,128)(2,1)} %reshape.1987), calls=%async_computation.1 | async-start | bytes 2097152 | tf_op jit(solution)/shard_map/all_to_all | solution.py:153
  183.0 7.5 %reshape.1992 = bf16[64,1,8192]{2,1,0:T(2,128)(2,1)} reshape(bf16[64,2,4096]{2,1,0:T(2,128)(2,1)} %all-to-all-done.3) | data formatting | bytes 2097152
  190.5 2.7 copy.212
  197.4 10.0 %all-to-all-done.1 = bf16[64,2,4096]{2,1,0:T(2,128)(2,1)} async-done(((bf16[64,2,4096]{2,1,0:T(2,128)(2,1)}), bf16[64,2,4096]{2,1,0:T(2,128)(2,1)}, u32[]{:S(2)}, u32[]{:S(2)}) %all-to-all-start.1) | async-done | bytes 1048608 | tf_op jit(solution)/shard_map/all_to_all | solution.py:153
  207.4 6.5 %reshape.1988 = bf16[64,1,8192]{2,1,0:T(2,128)(2,1)S(1)} reshape(bf16[64,2,4096]{2,1,0:T(2,128)(2,1)} %all-to-all-done.1) | data formatting | bytes 2097152
  229.5 106.6 %all-reduce.4 = (f32[128]{0:T(128)S(1)}, f32[128]{0:T(128)S(1)}) all-reduce(f32[128]{0:T(128)S(1)} %get-tuple-element.462, f32[128]{0:T(128)S(1)} %get-tuple-element.464), channel_id=1, replica_groups=mesh['shape'=4,'space'=64] {'space'}, use_global_device_ids=true, to_apply=%region_13.14 | all-reduce | flops 256 | bytes 2048 | tf_op jit(solution)/shard_map/psum | solution.py:243
  336.1 10.7 %all-reduce.6 = (f32[128]{0:T(128)S(1)}, f32[128]{0:T(128)S(1)}) all-reduce(f32[128]{0:T(128)S(1)} %get-tuple-element.466, f32[128]{0:T(128)S(1)} %get-tuple-element.467), channel_id=1, replica_groups=mesh['shape'=4,'space'=64] {'shape'}, use_global_device_ids=true, to_apply=%region_14.15 | all-reduce | flops 256 | bytes 2048 | tf_op jit(solution)/shard_map/psum | solution.py:242
  349.4 195.3 %all-reduce.11.cloned.1.call-done = (f32[7,128,128]{2,1,0:T(8,128)}, f32[7,128,128]{2,1,0:T(8,128)}) async-done(((f32[7,128,128]{2,1,0:T(8,128)}, f32[7,128,128]{2,1,0:T(8,128)}), (f32[7,128,128]{2,1,0:T(8,128)}, f32[7,128,128]{2,1,0:T(8,128)})) %all-reduce.11.cloned.1.call-update) | async-done | bytes 917520 | tf_op jit(solution)/shard_map/psum | solution.py:243
  547.6 47.8 %all-reduce.13.cloned.1.call-done = (f32[7,128,128]{2,1,0:T(8,128)}, f32[7,128,128]{2,1,0:T(8,128)}) async-done(((f32[7,128,128]{2,1,0:T(8,128)}, f32[7,128,128]{2,1,0:T(8,128)}), (f32[7,128,128]{2,1,0:T(8,128)}, f32[7,128,128]{2,1,0:T(8,128)})) %all-reduce.13.cloned.1.call-update) | async-done | bytes 917520 | tf_op jit(solution)/shard_map/psum | solution.py:242
  (254 shorter events, 106.8 us)
Async XLA Ops:
  9.7 2.7 copy-start.4
  9.8 2.3 copy-start.20
  9.8 2.5 copy-start.6
  9.9 2.5 copy-start.25
  16.4 12.6 %copy-start.29 = (s32[1,2]{1,0:T(1,128)S(1)}, s32[1,2]{1,0:T(1,128)}, u32[]{:S(2)}) copy-start(s32[1,2]{1,0:T(1,128)} %param.90) | copy-start | bytes 28
  16.4 12.6 %copy-start.9 = (bf16[1,2,512,128]{3,2,1,0:T(8,128)(2,1)S(1)}, bf16[1,2,512,128]{3,2,1,0:T(8,128)(2,1)}, u32[]{:S(2)}) copy-start(bf16[1,2,512,128]{3,2,1,0:T(8,128)(2,1)} %param.93) | copy-start | bytes 786436
  16.4 43.8 %all-to-all-start = ((bf16[64,2,4096]{2,1,0:T(2,128)(2,1)}), bf16[64,2,4096]{2,1,0:T(2,128)(2,1)}, u32[]{:S(2)}, u32[]{:S(2)}) async-start(bf16[64,2,4096]{2,1,0:T(2,128)(2,1)} %reshape.1985), calls=%async_computation | async-start | bytes 2097152 | tf_op jit(solution)/shard_map/all_to_all | solution.py:153
  31.1 2.9 copy-start.16
  46.7 5.7 copy-start.22
  60.2 37.6 %all-to-all-start.2 = ((bf16[64,2,4096]{2,1,0:T(2,128)(2,1)}), bf16[64,2,4096]{2,1,0:T(2,128)(2,1)}, u32[]{:S(2)}, u32[]{:S(2)}) async-start(bf16[64,2,4096]{2,1,0:T(2,128)(2,1)} %reshape.1989), calls=%async_computation.2 | async-start | bytes 2097152 | tf_op jit(solution)/shard_map/all_to_all | solution.py:171
  88.3 24.2 %copy-start.12 = (f32[2,8,8,8]{3,2,1,0:T(8,128)}, f32[2,8,8,8]{3,2,1,0:T(8,128)S(1)}, u32[]{:S(2)}) copy-start(f32[2,8,8,8]{3,2,1,0:T(8,128)S(1)} %div.59) | copy-start | bytes 12292
  88.8 23.7 %copy-start.13 = (f32[2,8,8,8]{3,2,1,0:T(8,128)}, f32[2,8,8,8]{3,2,1,0:T(8,128)S(1)}, u32[]{:S(2)}) copy-start(f32[2,8,8,8]{3,2,1,0:T(8,128)S(1)} %rsqrt.23) | copy-start | bytes 12292
  108.3 3.8 copy-start.27
  113.0 1.9 copy-start.15
  137.7 34.9 %all-to-all-start.3 = ((bf16[64,2,4096]{2,1,0:T(2,128)(2,1)}), bf16[64,2,4096]{2,1,0:T(2,128)(2,1)}, u32[]{:S(2)}, u32[]{:S(2)}) async-start(bf16[64,2,4096]{2,1,0:T(2,128)(2,1)} %reshape.1991), calls=%async_computation.3 | async-start | bytes 2097152 | tf_op jit(solution)/shard_map/all_to_all | solution.py:171
  146.0 2.1 copy-start.24
  146.0 2.8 copy-start.23
  157.9 2.0 copy-start.1
  172.5 34.9 %all-to-all-start.1 = ((bf16[64,2,4096]{2,1,0:T(2,128)(2,1)}), bf16[64,2,4096]{2,1,0:T(2,128)(2,1)}, u32[]{:S(2)}, u32[]{:S(2)}) async-start(bf16[64,2,4096]{2,1,0:T(2,128)(2,1)} %reshape.1987), calls=%async_computation.1 | async-start | bytes 2097152 | tf_op jit(solution)/shard_map/all_to_all | solution.py:153
  180.8 363.8 %all-reduce.11.cloned.1.call-start = ((), (), s32[]{:S(2)}) async-start(), calls=%async_computation.4 | async-start | bytes 1835008 | tf_op jit(solution)/shard_map/psum | solution.py:243
  226.5 2.8 copy-start.17
  229.3 118.8 %copy-start.8 = (bf16[2,8,8,8,128]{4,3,2,1,0:T(8,128)(2,1)S(1)}, bf16[2,8,8,8,128]{4,3,2,1,0:T(8,128)(2,1)}, u32[]{:S(2)}) copy-start(bf16[2,8,8,8,128]{4,3,2,1,0:T(8,128)(2,1)} %get-tuple-element.480) | copy-start | bytes 786436
  346.9 248.5 %all-reduce.13.cloned.1.call-start = ((), (), s32[]{:S(2)}) async-start(), calls=%async_computation.5 | async-start | bytes 1835008 | tf_op jit(solution)/shard_map/psum | solution.py:242
  349.2 196.3 %copy-start.3 = (bf16[1,2,512,128]{3,2,1,0:T(8,128)(2,1)S(1)}, bf16[1,2,512,128]{3,2,1,0:T(8,128)(2,1)}, u32[]{:S(2)}) copy-start(bf16[1,2,512,128]{3,2,1,0:T(8,128)(2,1)} %param.85) | copy-start | bytes 786436
  (12 other events, 14.0 us)
Sparse Core Ops, SparseCore 0:
  347.0 197.6 all-reduce.10
  547.2 48.1 all-reduce.12
